TPU v7x, 256 devices: a whole 4x4x8 slice. The times are simulated.
256 devices in a mesh: ctx: 32 (over y, x, core), head: 8 (over z).
Axes of the slice: x: 4, y: 4, z: 8, core: 2. Of those that a mesh axis runs over, the one named last changes fastest.
Arguments:
- queries: bfloat16 [32768, 4096], P(('ctx', 'head')), may hold values from -8 to 8
- key_vectors: bfloat16 [32768, 4096], P(('ctx', 'head')), may hold values from -8 to 8
- value_vectors: bfloat16 [32768, 4096], P(('ctx', 'head')), may hold values from -6 to 6
- out_grad: bfloat16 [32768, 4096], P(('ctx', 'head')), may hold values from -6 to 6
- doc_ids: int32 [256], P('ctx'), may hold values from 0 to 15, as said below
Outputs:
- attended: bfloat16 [32768, 4096], P(('ctx', 'head'))
- query_grad: bfloat16 [32768, 4096], P(('ctx', 'head'))
- key_grad: bfloat16 [32768, 4096], P(('ctx', 'head'))
- value_grad: bfloat16 [32768, 4096], P(('ctx', 'head'))
Inputs may be any that keep to these rules, and one draw needn't show every extreme that they name: `doc_ids`: document numbers never fall along the stretches and every number is used. Document 0 has exactly 96 stretches, no document has more, and the last document has more than 8 stretches.
All inputs are finite; a program needn't handle non-finite values.
Results may differ from a plain program's by a relative error of at most 0.0095.
Values may be sent and summed in bfloat16 or wider, within the bound.
A program may use at most 128 MiB of HBM per device.

v0:
```python
import jax
import jax.numpy as jnp
from jax import lax
from jax.sharding import PartitionSpec as P

HD = 128
STRETCH = 128


def prefix_2(value, axis, join, neutral):
    count, mine = (lax.axis_size(axis), lax.axis_index(axis))
    pieces = jax.tree.map(lambda part: lax.all_gather(part, axis), value)
    so_far = jax.tree.map(
        lambda part, zero: jnp.full_like(part, 0) + jnp.asarray(zero, part.dtype), value, neutral
    )

    def lap(position, so_far):
        longer = join(so_far, jax.tree.map(lambda part: part[position], pieces))
        return jax.tree.map(lambda new, old: jnp.where(position < mine, new, old), longer, so_far)

    return lax.fori_loop(0, count - 1, lap, so_far)


def prefix_3(array, axis, join, neutral):
    count = lax.axis_size(axis)
    place = lax.axis_index(axis)
    ahead = count - 1 - place
    gathered = jax.tree.map(
        lambda a, kind: lax.all_gather(a.astype(kind), axis), array, (jnp.bfloat16, jnp.bfloat16)
    )
    state = jax.tree.map(lambda a, e: jnp.zeros_like(a) + jnp.asarray(e, a.dtype), array, neutral)

    def one(lap, state):
        source = count - 1 - lap
        return join(
            state,
            jax.tree.map(
                lambda a, own: lax.dynamic_index_in_dim(a, source, 0, False).astype(own.dtype),
                gathered,
                array,
            ),
        )

    return lax.fori_loop(0, ahead, one, state)


def feature_map(values):
    wide = values.astype(jnp.float32)
    return jnp.where(wide > 0, wide + 1.0, jnp.exp(jnp.minimum(wide, 0.0)))


def feature_slope(values):
    wide = values.astype(jnp.float32)
    return jnp.where(wide > 0, jnp.ones_like(wide), jnp.exp(jnp.minimum(wide, 0.0)))


def exact(form, left, right):
    return jnp.einsum(form, left, right, precision=lax.Precision.HIGHEST)


def state_product(form, data_half, state):
    high_part = state.astype(jnp.bfloat16)
    rest = state - lax.optimization_barrier(high_part).astype(jnp.float32)
    low_part = rest.astype(jnp.bfloat16)
    first = jnp.einsum(form, data_half, high_part, preferred_element_type=jnp.float32)
    second = jnp.einsum(form, data_half, low_part, preferred_element_type=jnp.float32)
    return first + second


def join_forward(earlier, later):
    keep = earlier[1] >= later[1]
    return (later[0] + jnp.where(keep, earlier[0], 0.0), jnp.maximum(earlier[1], later[1]))


def join_backward(earlier, later):
    keep = earlier[1] <= later[1]
    return (later[0] + jnp.where(keep, earlier[0], 0.0), jnp.minimum(earlier[1], later[1]))


def local_part(pieces, doc_ids):
    queries, key_vectors, value_vectors, out_grad = pieces
    tokens = queries.shape[0]
    heads = queries.shape[2]
    count = tokens // STRETCH

    def blocked(array):
        return array.reshape(count, STRETCH, heads, HD)

    query_block = blocked(queries)
    key_block = blocked(key_vectors)
    query_half = feature_map(query_block).astype(jnp.bfloat16)
    key_half = feature_map(key_block).astype(jnp.bfloat16)
    value_half = blocked(value_vectors)
    grad_wide = blocked(out_grad).astype(jnp.float32)
    stretch_ids = doc_ids.astype(jnp.float32)
    order = jnp.arange(count)
    same = stretch_ids[:, None] == stretch_ids[None, :]
    earlier_mask = (same & (order[None, :] < order[:, None])).astype(jnp.float32)
    later_mask = (same & (order[None, :] > order[:, None])).astype(jnp.float32)
    causal = (jnp.arange(STRETCH)[:, None] >= jnp.arange(STRETCH)[None, :])[None, None]
    scores = jnp.where(
        causal,
        jnp.einsum("ntha,nsha->nhts", query_half, key_half, preferred_element_type=jnp.float32),
        0.0,
    ).astype(jnp.bfloat16)
    pair_states = jnp.einsum(
        "nsha,nshb->nhab", key_half, value_half, preferred_element_type=jnp.float32
    )
    last_id = stretch_ids[count - 1]
    summary = exact("d,dhab->hab", (stretch_ids == last_id).astype(jnp.float32), pair_states)
    carried, carried_last = prefix_2(
        (summary, last_id),
        "ctx",
        join_forward,
        (jnp.zeros_like(summary), jnp.array(-1.0, jnp.float32)),
    )
    incoming = jnp.where((stretch_ids == carried_last)[:, None, None, None], carried[None], 0.0)
    prefix = exact("cd,dhab->chab", earlier_mask, pair_states) + incoming
    raw = jnp.einsum(
        "nhts,nshb->nthb", scores, value_half, preferred_element_type=jnp.float32
    ) + state_product("ntha,nhab->nthb", query_half, prefix)
    rms_scale = jnp.sqrt(jnp.mean(raw * raw, axis=-1, keepdims=True) + 1e-06)
    normed = raw / rms_scale
    along = jnp.mean(grad_wide * normed, axis=-1, keepdims=True)
    scaled = ((grad_wide - normed * along) / rms_scale).astype(jnp.bfloat16)
    mixed = jnp.where(
        causal,
        jnp.einsum("nthb,nshb->nhts", scaled, value_half, preferred_element_type=jnp.float32),
        0.0,
    ).astype(jnp.bfloat16)
    query_states = jnp.einsum(
        "ntha,nthb->nhab", query_half, scaled, preferred_element_type=jnp.float32
    )
    first_id = stretch_ids[0]
    summary_back = exact("d,dhab->hab", (stretch_ids == first_id).astype(jnp.float32), query_states)
    carried_back, carried_first = prefix_3(
        (summary_back, first_id),
        "ctx",
        join_backward,
        (jnp.zeros_like(summary_back), jnp.array(1000000000.0, jnp.float32)),
    )
    incoming_back = jnp.where(
        (stretch_ids == carried_first)[:, None, None, None], carried_back[None], 0.0
    )
    suffix = exact("cd,dhab->chab", later_mask, query_states) + incoming_back
    query_grad = (
        jnp.einsum("nhts,nsha->ntha", mixed, key_half, preferred_element_type=jnp.float32)
        + state_product("nthb,nhab->ntha", scaled, prefix)
    ) * feature_slope(query_block)
    key_grad = (
        jnp.einsum("nhts,ntha->nsha", mixed, query_half, preferred_element_type=jnp.float32)
        + state_product("nshb,nhab->nsha", value_half, suffix)
    ) * feature_slope(key_block)
    value_grad = jnp.einsum(
        "nhts,nthb->nshb", scores, scaled, preferred_element_type=jnp.float32
    ) + state_product("nsha,nhab->nshb", key_half, suffix)

    def unblocked(array):
        return array.reshape(tokens, 1, heads, HD).astype(jnp.bfloat16)

    return (unblocked(normed), unblocked(query_grad), unblocked(key_grad), unblocked(value_grad))


def shards(queries, key_vectors, value_vectors, out_grad, doc_ids):
    groups = lax.axis_size("head")
    rows = queries.shape[0]
    heads_all = queries.shape[1] // HD
    local_heads = heads_all // groups

    def grouped(array):
        return array.reshape(rows, groups, local_heads, HD)

    results = local_part(
        (
            lax.all_to_all(grouped(queries), "head", split_axis=1, concat_axis=0, tiled=True),
            lax.all_to_all(grouped(key_vectors), "head", split_axis=1, concat_axis=0, tiled=True),
            lax.all_to_all(grouped(value_vectors), "head", split_axis=1, concat_axis=0, tiled=True),
            lax.all_to_all(grouped(out_grad), "head", split_axis=1, concat_axis=0, tiled=True),
        ),
        doc_ids=doc_ids,
    )
    returned = (
        lax.all_to_all(results[0], "head", split_axis=0, concat_axis=1, tiled=True),
        lax.all_to_all(results[1], "head", split_axis=0, concat_axis=1, tiled=True),
        lax.all_to_all(results[2], "head", split_axis=0, concat_axis=1, tiled=True),
        lax.all_to_all(results[3], "head", split_axis=0, concat_axis=1, tiled=True),
    )

    def flat(array):
        return array.reshape(rows, heads_all * HD)

    return (flat(returned[0]), flat(returned[1]), flat(returned[2]), flat(returned[3]))


def solution(mesh):
    in_specs = (
        P(("ctx", "head"), None),
        P(("ctx", "head"), None),
        P(("ctx", "head"), None),
        P(("ctx", "head"), None),
        P("ctx"),
    )
    out_specs = (
        P(("ctx", "head"), None),
        P(("ctx", "head"), None),
        P(("ctx", "head"), None),
        P(("ctx", "head"), None),
    )
    return jax.shard_map(shards, mesh=mesh, in_specs=in_specs, out_specs=out_specs, check_vma=False)
```

profile of v0, /device:TPU:32, one launch (start us, length us, event | category | flops | bytes accessed | tf_op | source)
XLA Modules:
  0.0 564.9 jit_solution(3951862314442988401)
XLA Ops:
  10.1 8.6 %all-to-all-start.2 = ((bf16[128,8,4,128]{3,0,2,1:T(8,128)(2,1)}), bf16[128,8,4,128]{3,0,2,1:T(8,128)(2,1)S(1)}, u32[]{:S(2)}, u32[]{:S(2)}) async-start(bf16[128,8,4,128]{3,0,2,1:T(8,128)(2,1)} %copy.70), calls=%async_computation.2 | async-start | bytes 2097152 | tf_op jit(solution)/shard_map/all_to_all | solution.py:177
  20.7 25.3 %all-to-all-done.2 = bf16[128,8,4,128]{3,0,2,1:T(8,128)(2,1)S(1)} async-done(((bf16[128,8,4,128]{3,0,2,1:T(8,128)(2,1)}), bf16[128,8,4,128]{3,0,2,1:T(8,128)(2,1)S(1)}, u32[]{:S(2)}, u32[]{:S(2)}) %all-to-all-start.2) | async-done | bytes 1048608 | tf_op jit(solution)/shard_map/all_to_all | solution.py:177
  46.0 4.9 all-to-all-start.1
  52.8 25.9 %all-to-all-done.1 = bf16[128,8,4,128]{3,0,2,1:T(8,128)(2,1)S(1)} async-done(((bf16[128,8,4,128]{3,0,2,1:T(8,128)(2,1)}), bf16[128,8,4,128]{3,0,2,1:T(8,128)(2,1)S(1)}, u32[]{:S(2)}, u32[]{:S(2)}) %all-to-all-start.1) | async-done | bytes 1048608 | tf_op jit(solution)/shard_map/all_to_all | solution.py:176
  80.8 3.5 fusion.22
  87.3 5.6 all-to-all-start
  95.8 68.3 %all-reduce = f32[32]{0:T(128)S(1)} all-reduce(f32[32]{0:T(128)S(1)} %get-tuple-element.255), channel_id=1, replica_groups=mesh['ctx'=32,'head'=8] {'ctx'}, use_global_device_ids=true, to_apply=%add | all-reduce | flops 32 | bytes 256
  164.1 6.9 %all-to-all-start.4 = ((bf16[128,8,4,128]{3,0,2,1:T(8,128)(2,1)}), bf16[128,8,4,128]{3,0,2,1:T(8,128)(2,1)}, u32[]{:S(2)}, u32[]{:S(2)}) async-start(bf16[128,8,4,128]{3,0,2,1:T(8,128)(2,1)} %copy.79), calls=%async_computation.4 | async-start | bytes 2097152 | tf_op jit(solution)/shard_map/all_to_all | solution.py:178
  171.0 2.5 select_convert_fusion.1
  173.6 1.8 fusion.37
  176.3 2.2 fusion.24
  178.5 91.7 %while.31 = (s32[]{:T(128)}, f32[4,128,128]{2,1,0:T(8,128)S(1)}, f32[]{:T(128)}, s32[]{:T(128)}, f32[32,4,128,128]{3,2,1,0:T(8,128)}, /*index=5*/f32[32]{0:T(128)S(1)}, s32[]{:T(128)}, s32[]{:T(128)}) while((s32[]{:T(128)}, f32[4,128,128]{2,1,0:T(8,128)S(1)}, f32[]{:T(128)}, s32[]{:T(128)}, f32[32,4,128,128]{3,2,1,0:T(8,128)}, ...), condition=%wide.region_1.2_spmd.clone, body=%wide.region_0.1_spmd.clone.sunk | while | flops 262151 | bytes 786596 | solution.py:21
  270.8 2.2 fusion.60
  274.7 2.6 multiply_reduce_fusion
  277.3 2.7 fusion.15
  280.1 2.7 fusion.17
  282.7 2.0 fusion.56
  286.1 2.8 fusion.18
  290.9 63.0 %all-reduce.1 = bf16[32]{0:T(256)(128)(2,1)S(1)} all-reduce(bf16[32]{0:T(256)(128)(2,1)S(1)} %dynamic-update-slice.1), channel_id=1, replica_groups=mesh['ctx'=32,'head'=8] {'ctx'}, use_global_device_ids=true, to_apply=%add.1 | all-reduce | flops 32 | bytes 128
  355.8 7.3 %all-to-all-start.3 = ((bf16[1024,1,4,128]{3,2,1,0:T(4,128)(2,1)}), bf16[1024,1,4,128]{3,2,1,0:T(4,128)(2,1)}, u32[]{:S(2)}, u32[]{:S(2)}) async-start(bf16[1024,1,4,128]{3,2,1,0:T(4,128)(2,1)} %copy.75), calls=%async_computation.3 | async-start | bytes 2097152 | tf_op jit(solution)/shard_map/all_to_all | solution.py:183
  366.4 2.6 fusion.7
  370.9 3.6 fusion.58
  374.5 3.6 fusion.20
  378.1 12.8 %all-to-all-done.3 = bf16[1024,1,4,128]{3,2,1,0:T(4,128)(2,1)} async-done(((bf16[1024,1,4,128]{3,2,1,0:T(4,128)(2,1)}), bf16[1024,1,4,128]{3,2,1,0:T(4,128)(2,1)}, u32[]{:S(2)}, u32[]{:S(2)}) %all-to-all-start.3) | async-done | bytes 1048608 | tf_op jit(solution)/shard_map/all_to_all | solution.py:183
  390.9 5.6 all-to-all-start.5
  396.5 90.0 %while.30 = (s32[]{:T(128)}, f32[4,128,128]{2,1,0:T(8,128)S(1)}, f32[]{:T(128)}, s32[]{:T(128)}, bf16[32,4,128,128]{3,2,1,0:T(8,128)(2,1)}, /*index=5*/bf16[32]{...) while((s32[]{:T(128)}, f32[4,128,128]{2,1,0:T(8,128)S(1)}, f32[]{:T(128)}, s32[]{:T(128)}, ...), condition=%wide.region_5.6_spmd, body=%wide.region_4.5_spmd.sunk | while | flops 196616 | bytes 655545 | solution.py:44
  486.6 2.1 fusion.27
  495.1 7.2 %all-to-all-start.6 = ((bf16[1024,1,4,128]{3,2,1,0:T(4,128)(2,1)}), bf16[1024,1,4,128]{3,2,1,0:T(4,128)(2,1)}, u32[]{:S(2)}, u32[]{:S(2)}) async-start(bf16[1024,1,4,128]{3,2,1,0:T(4,128)(2,1)} %copy.89), calls=%async_computation.6 | async-start | bytes 2097152 | tf_op jit(solution)/shard_map/all_to_all | solution.py:185
  502.3 1.8 fusion.73
  508.1 18.7 %all-to-all-done.6 = bf16[1024,1,4,128]{3,2,1,0:T(4,128)(2,1)} async-done(((bf16[1024,1,4,128]{3,2,1,0:T(4,128)(2,1)}), bf16[1024,1,4,128]{3,2,1,0:T(4,128)(2,1)}, u32[]{:S(2)}, u32[]{:S(2)}) %all-to-all-start.6) | async-done | bytes 1048608 | tf_op jit(solution)/shard_map/all_to_all | solution.py:185
  526.7 4.9 all-to-all-start.7
  541.7 14.2 %all-to-all-done.7 = bf16[1024,1,4,128]{3,2,1,0:T(4,128)(2,1)S(1)} async-done(((bf16[1024,1,4,128]{3,2,1,0:T(4,128)(2,1)}), bf16[1024,1,4,128]{3,2,1,0:T(4,128)(2,1)S(1)}, u32[]{:S(2)}, u32[]{:S(2)}) %all-to-all-start.7) | async-done | bytes 1048608 | tf_op jit(solution)/shard_map/all_to_all | solution.py:186
  (230 shorter events, 149.2 us)
Async XLA Ops:
  8.8 9.9 %copy-start.19 = (bf16[128,4096]{1,0:T(8,128)(2,1)S(1)}, bf16[128,4096]{1,0:T(8,128)(2,1)}, u32[]{:S(2)}) copy-start(bf16[128,4096]{1,0:T(8,128)(2,1)} %param.10) | copy-start | bytes 3145732
  10.1 35.8 %all-to-all-start.2 = ((bf16[128,8,4,128]{3,0,2,1:T(8,128)(2,1)}), bf16[128,8,4,128]{3,0,2,1:T(8,128)(2,1)S(1)}, u32[]{:S(2)}, u32[]{:S(2)}) async-start(bf16[128,8,4,128]{3,0,2,1:T(8,128)(2,1)} %copy.70), calls=%async_computation.2 | async-start | bytes 2097152 | tf_op jit(solution)/shard_map/all_to_all | solution.py:177
  19.3 31.5 %copy-start.20 = (s32[8]{0:T(128)S(1)}, s32[8]{0:T(128)}, u32[]{:S(2)}) copy-start(s32[8]{0:T(128)} %param.13) | copy-start | bytes 100
  19.4 31.6 %copy-start.21 = (u32[256]{0:T(256)S(1)}, u32[256]{0:T(256)}, u32[]{:S(2)}) copy-start(u32[256]{0:T(256)} %constant.94) | copy-start | bytes 3076
  46.0 32.7 %all-to-all-start.1 = ((bf16[128,8,4,128]{3,0,2,1:T(8,128)(2,1)}), bf16[128,8,4,128]{3,0,2,1:T(8,128)(2,1)S(1)}, u32[]{:S(2)}, u32[]{:S(2)}) async-start(bf16[128,8,4,128]{3,0,2,1:T(8,128)(2,1)} %copy.68), calls=%async_computation.1 | async-start | bytes 2097152 | tf_op jit(solution)/shard_map/all_to_all | solution.py:176
  50.9 127.7 %all-gather.5.cloned.1.call-start = ((), (), s32[]{:S(2)}) async-start(), calls=%async_computation.8 | async-start | bytes 8650752 | tf_op jit(solution)/shard_map/all_gather | solution.py:12
  78.6 92.4 %copy-start.6 = (bf16[128,8,4,128]{3,0,2,1:T(8,128)(2,1)}, bf16[128,8,4,128]{3,0,2,1:T(8,128)(2,1)S(1)}, u32[]{:S(2)}) copy-start(bf16[128,8,4,128]{3,0,2,1:T(8,128)(2,1)S(1)} %all-to-all-done.1) | copy-start | bytes 3145732
  79.4 1.4 copy-start.14
  87.3 76.9 %all-to-all-start = ((bf16[128,8,4,128]{3,0,2,1:T(8,128)(2,1)}), bf16[128,8,4,128]{3,0,2,1:T(8,128)(2,1)}, u32[]{:S(2)}, u32[]{:S(2)}) async-start(bf16[128,8,4,128]{3,0,2,1:T(8,128)(2,1)} %copy.66), calls=%async_computation | async-start | bytes 2097152 | tf_op jit(solution)/shard_map/all_to_all | solution.py:175
  164.1 113.1 %all-to-all-start.4 = ((bf16[128,8,4,128]{3,0,2,1:T(8,128)(2,1)}), bf16[128,8,4,128]{3,0,2,1:T(8,128)(2,1)}, u32[]{:S(2)}, u32[]{:S(2)}) async-start(bf16[128,8,4,128]{3,0,2,1:T(8,128)(2,1)} %copy.79), calls=%async_computation.4 | async-start | bytes 2097152 | tf_op jit(solution)/shard_map/all_to_all | solution.py:178
  171.0 225.4 %all-gather.7.cloned.1.call-start = ((), (), s32[]{:S(2)}) async-start(), calls=%async_computation.9 | async-start | bytes 4325376 | tf_op jit(solution)/shard_map/all_gather | solution.py:29
  173.6 1.9 copy-start.17
  173.6 2.7 copy-start.15
  270.8 2.3 copy-start.2
  273.1 1.6 copy-start.16
  274.7 2.6 copy-start.10
  277.3 2.8 copy-start.1
  284.7 1.4 copy-start.12
  354.1 9.1 %copy-start.3 = (bf16[8,4,128,128]{3,2,1,0:T(8,128)(2,1)S(1)}, bf16[8,4,128,128]{3,2,1,0:T(8,128)(2,1)}, u32[]{:S(2)}) copy-start(bf16[8,4,128,128]{3,2,1,0:T(8,128)(2,1)} %copy-done.2) | copy-start | bytes 3145732
  355.8 35.0 %all-to-all-start.3 = ((bf16[1024,1,4,128]{3,2,1,0:T(4,128)(2,1)}), bf16[1024,1,4,128]{3,2,1,0:T(4,128)(2,1)}, u32[]{:S(2)}, u32[]{:S(2)}) async-start(bf16[1024,1,4,128]{3,2,1,0:T(4,128)(2,1)} %copy.75), calls=%async_computation.3 | async-start | bytes 2097152 | tf_op jit(solution)/shard_map/all_to_all | solution.py:183
  363.9 1.2 copy-start.11
  365.2 1.2 copy-start.7
  370.9 3.6 copy-start.13
  390.9 104.3 %all-to-all-start.5 = ((bf16[1024,1,4,128]{3,2,1,0:T(4,128)(2,1)}), bf16[1024,1,4,128]{3,2,1,0:T(4,128)(2,1)}, u32[]{:S(2)}, u32[]{:S(2)}) async-start(bf16[1024,1,4,128]{3,2,1,0:T(4,128)(2,1)} %copy.81), calls=%async_computation.5 | async-start | bytes 2097152 | tf_op jit(solution)/shard_map/all_to_all | solution.py:184
  488.7 1.6 copy-start
  490.3 1.2 copy-start.8
  490.3 1.9 copy-start.18
  492.2 1.1 copy-start.4
  495.1 31.6 %all-to-all-start.6 = ((bf16[1024,1,4,128]{3,2,1,0:T(4,128)(2,1)}), bf16[1024,1,4,128]{3,2,1,0:T(4,128)(2,1)}, u32[]{:S(2)}, u32[]{:S(2)}) async-start(bf16[1024,1,4,128]{3,2,1,0:T(4,128)(2,1)} %copy.89), calls=%async_computation.6 | async-start | bytes 2097152 | tf_op jit(solution)/shard_map/all_to_all | solution.py:185
  502.3 1.8 copy-start.9
  504.2 1.2 copy-start.5
  526.7 29.2 %all-to-all-start.7 = ((bf16[1024,1,4,128]{3,2,1,0:T(4,128)(2,1)}), bf16[1024,1,4,128]{3,2,1,0:T(4,128)(2,1)S(1)}, u32[]{:S(2)}, u32[]{:S(2)}) async-start(bf16[1024,1,4,128]{3,2,1,0:T(4,128)(2,1)} %copy.94), calls=%async_computation.7 | async-start | bytes 2097152 | tf_op jit(solution)/shard_map/all_to_all | solution.py:186
Sparse Core Ops, SparseCore 0:
  84.4 55.4 all-gather.4
  289.7 47.2 all-gather.6
where the time goes:
time: 569 us; the launch traced here: 565 us
  blocking collectives  131 us (23%)
  waiting for transfers between devices  96.9 us (17%)
  loops' own time  82.7 us (15%)
  local copies, waits for them, and re-layouts  77.4 us (14%)
  other arithmetic  72.6 us (13%)
  starting transfers between devices  51 us (9%)
  matrix products  37.9 us (7%)
  between operations  15.1 us (3%)
    unnamed x2, blocking collectives  131 us
    another operation x1, loops' own time, prefix_3(): return lax.fori_loop(0, ahead, one, state)  41.4 us
    another operation x1, loops' own time, prefix_2(): return lax.fori_loop(0, count - 1, lap, so_far)  41.3 us
    select_n x31, other arithmetic, lap(): jnp.where(position < mine, new, old)  32.2 us
    add x31, other arithmetic, join_backward(): later[0] + jnp.where(keep, earlier[0], 0.0)  30.5 us
    all_to_all x1, waiting for transfers between devices, shards(): lax.all_to_all(grouped(key_vectors), 'head', split_axis=1, concat_axis=0,...  25.9 us
    all_to_all x1, waiting for transfers between devices, shards(): lax.all_to_all(grouped(value_vectors), 'head', split_axis=1, concat_axis=...  25.3 us
    unnamed x56, local copies, waits for them, and re-layouts  20.2 us
  transfers between devices with their start and end apart: 10, of which 5 were waited for; matrix products, arithmetic and copies ran while one was open for 28% of the time, Pallas kernels for 0%

commit v1 on v0

v1 whole, which is shorter than its diff:
```python
import functools

import jax
import jax.numpy as jnp
from jax import lax
from jax.experimental import pallas as pl
from jax.experimental.pallas import tpu as pltpu
from jax.sharding import PartitionSpec as P

HD = 128
TAG = 16
MESH = pl.DeviceIdType.MESH
F32 = jnp.float32
BF16 = jnp.bfloat16


def feature(x):
    return jnp.where(x > 0, x + 1.0, jnp.exp(jnp.minimum(x, 0.0)))


def slope(x):
    return jnp.where(x > 0, jnp.ones_like(x), jnp.exp(jnp.minimum(x, 0.0)))


def dot_nn(a, b):
    return lax.dot_general(a, b, (((1,), (0,)), ((), ())), preferred_element_type=F32)


def dot_nt(a, b):
    return lax.dot_general(a, b, (((1,), (1,)), ((), ())), preferred_element_type=F32)


def dot_tn(a, b):
    return lax.dot_general(a, b, (((0,), (0,)), ((), ())), preferred_element_type=F32)


def kernel(
    ny,
    nx,
    nz,
    chunks,
    ids,
    q_ref,
    k_ref,
    v_ref,
    g_ref,
    att_ref,
    qg_ref,
    kg_ref,
    vg_ref,
    kf_buf,
    qf_buf,
    a_buf,
    sc_buf,
    kl_buf,
    vl_buf,
    s_out,
    s_in,
    p_out,
    p_in,
    g_out,
    g_in,
    t_out,
    t_in,
    u_out,
    u_in,
    send_a,
    recv_a,
    send_g,
    recv_g,
    send_t,
    recv_t,
    send_u,
    recv_u,
):
    ctx = lax.axis_index("ctx")
    z = lax.axis_index("head")
    core = lax.rem(ctx, 2)
    x = lax.rem(ctx // 2, nx)
    y = ctx // (2 * nx)

    def at(yy, xx, cc):
        return (yy * nx + xx) * 2 + cc

    peer = (at(y, x, 1 - core), z)
    lines = [(ctx, lax.rem(z + d, nz)) for d in range(1, nz)]
    rows = [(at(y, lax.rem(x + d, nx), core), z) for d in range(1, nx)]
    columns = [(at(lax.rem(y + d, ny), x, core), z) for d in range(1, ny)]
    everyone = lines + rows + columns + [peer]

    barrier = pltpu.get_barrier_semaphore()
    for device in everyone:
        pl.semaphore_signal(barrier, inc=1, device_id=device, device_id_type=MESH)

    core_one = (core == 1).astype(F32)
    doc = [ids[i] for i in range(nz)]
    causal = lax.broadcasted_iota(jnp.int32, (HD, HD), 0) >= lax.broadcasted_iota(
        jnp.int32, (HD, HD), 1
    )

    def alike(a, b):
        return jnp.where(a == b, 1.0, 0.0).astype(F32)

    def columns_of(h):
        return pl.ds(pl.multiple_of(h * HD, HD), HD)

    def remote(src, dst, send, recv, device):
        return pltpu.make_async_remote_copy(
            src_ref=src,
            dst_ref=dst,
            send_sem=send,
            recv_sem=recv,
            device_id=device,
            device_id_type=MESH,
        )

    def exchange(out, into, phase, j):
        into[j, z] = out[j, z]
        for device in lines:
            remote(
                out.at[j, device[1]],
                into.at[j, z],
                send_a.at[phase, j],
                recv_a.at[phase, j],
                device,
            ).start()

    def wait_in(into, sem, count):
        part = into.at[pl.ds(0, count)]
        pltpu.make_async_copy(part, part, sem).wait()

    def heads(body):
        def pair(i, carry):
            for u in range(2):
                body(i * 2 + u)
            return carry

        lax.fori_loop(0, nz // 2, pair, 0)

    def states(j):
        def one(o):
            h = nz * j + o
            c = columns_of(h)
            kf = feature(k_ref[:, c].astype(F32)).astype(BF16)
            kf_buf[h] = kf
            s_out[0, j, o] = dot_tn(kf, v_ref[:, c]).astype(BF16)

        heads(one)

    def before(j):
        def one(o):
            h = nz * j + o
            c = columns_of(h)
            qf = feature(q_ref[:, c].astype(F32)).astype(BF16)
            qf_buf[h] = qf
            a_buf[h] = jnp.where(causal, dot_nt(qf, kf_buf[h]), 0.0).astype(BF16)

        heads(one)

    def tag_of(message):
        return message[pl.ds(HD, TAG), :].astype(F32)[0:1, :]

    def value_of(message):
        return message[pl.ds(0, HD), :].astype(F32)

    def put(message, value, tag):
        message[pl.ds(0, HD), :] = value.astype(BF16)
        message[pl.ds(HD, TAG), :] = jnp.broadcast_to(tag, (TAG, HD)).astype(BF16)

    def group_sum(way, j):
        wait_in(s_in.at[way, j], recv_a.at[2 * way, j], nz - 1)
        edge = doc[nz - 1] if way == 0 else doc[0]
        total = jnp.zeros((HD, HD), F32)
        for i in range(nz):
            total = total + alike(doc[i], edge) * s_in[way, j, i].astype(F32)
        put(g_out.at[way, j], total, edge.astype(F32) * jnp.ones((1, HD), F32))
        remote(
            g_out.at[way, j], g_in.at[way, j], send_g.at[way, j], recv_g.at[way, j], peer
        ).start()

    def chip_sum(way, j):
        pltpu.make_async_copy(g_in.at[way, j], g_in.at[way, j], recv_g.at[way, j]).wait()
        mine, other = g_out.at[way, j], g_in.at[way, j]
        late = core_one if way == 0 else 1.0 - core_one
        same = alike(tag_of(mine), tag_of(other))
        keep_mine = late + (1.0 - late) * same
        keep_other = (1.0 - late) + late * same
        put(
            t_out.at[way, j],
            keep_mine * value_of(mine) + keep_other * value_of(other),
            late * tag_of(mine) + (1.0 - late) * tag_of(other),
        )
        for d, device in enumerate(rows):
            remote(
                t_out.at[way, j],
                t_in.at[way, j, d],
                send_t.at[way, j],
                recv_t.at[way, j],
                device,
            ).start()

    def row_sum(way, j):
        wait_in(t_in.at[way, j], recv_t.at[way, j], nx - 1)
        edge = nx - 1 if way == 0 else 0
        parts = [(t_out.at[way, j], x)] + [
            (t_in.at[way, j, d], lax.rem(x + nx - 1 - d, nx)) for d in range(nx - 1)
        ]
        tag = jnp.zeros((1, HD), F32)
        for part, place in parts:
            tag = tag + alike(place, edge) * tag_of(part)
        total = jnp.zeros((HD, HD), F32)
        for part, place in parts:
            total = total + alike(tag_of(part), tag) * value_of(part)
        put(u_out.at[way, j], total, tag)
        for d, device in enumerate(columns):
            remote(
                u_out.at[way, j],
                u_in.at[way, j, d],
                send_u.at[way, j],
                recv_u.at[way, j],
                device,
            ).start()

    def hand_back(way, j):
        wait_in(u_in.at[way, j], recv_u.at[way, j], ny - 1)
        want = (doc[0] if way == 0 else doc[nz - 1]).astype(F32)
        late = core_one if way == 0 else 1.0 - core_one
        other = g_in.at[way, j]
        running = late * alike(tag_of(other), want) * value_of(other)
        for d in range(nx - 1):
            before_me = (x >= d + 1) if way == 0 else (x < d + 1)
            part = t_in.at[way, j, d]
            running = running + before_me.astype(F32) * alike(tag_of(part), want) * value_of(part)
        for d in range(ny - 1):
            before_me = (y >= d + 1) if way == 0 else (y < d + 1)
            part = u_in.at[way, j, d]
            running = running + before_me.astype(F32) * alike(tag_of(part), want) * value_of(part)
        order = list(range(nz)) if way == 0 else list(range(nz - 1, -1, -1))
        for n, i in enumerate(order):
            p_out[way, j, i] = running.astype(BF16)
            if n < nz - 1:
                running = alike(doc[i], doc[order[n + 1]]) * (
                    running + s_in[way, j, i].astype(F32)
                )
        exchange(p_out.at[way], p_in.at[way], 2 * way + 1, j)

    def middle(j):
        wait_in(p_in.at[0, j], recv_a.at[1, j], nz - 1)

        def one(o):
            h = nz * j + o
            c = columns_of(h)
            qf = qf_buf[h]
            raw = dot_nn(a_buf[h], v_ref[:, c]) + dot_nn(qf, p_in[0, j, o])
            inverse = lax.rsqrt(jnp.mean(raw * raw, axis=-1, keepdims=True) + 1e-06)
            normed = raw * inverse
            att_ref[:, c] = normed.astype(BF16)
            wide = g_ref[:, c].astype(F32)
            along = jnp.mean(wide * normed, axis=-1, keepdims=True)
            scaled = ((wide - normed * along) * inverse).astype(BF16)
            sc_buf[h] = scaled
            s_out[1, j, o] = dot_tn(qf, scaled).astype(BF16)

        heads(one)
        exchange(s_out.at[1], s_in.at[1], 2, j)

    def after(j):
        def one(o):
            h = nz * j + o
            c = columns_of(h)
            scaled = sc_buf[h]
            mixed = jnp.where(causal, dot_nt(scaled, v_ref[:, c]), 0.0).astype(BF16)
            grad = dot_nn(mixed, kf_buf[h]) + dot_nt(scaled, p_in[0, j, o])
            qg_ref[:, c] = (grad * slope(q_ref[:, c].astype(F32))).astype(BF16)
            kl_buf[h] = dot_tn(mixed, qf_buf[h])
            vl_buf[h] = dot_tn(a_buf[h], scaled)

        heads(one)

    def finish(j):
        wait_in(p_in.at[1, j], recv_a.at[3, j], nz - 1)

        def one(o):
            h = nz * j + o
            c = columns_of(h)
            state = p_in[1, j, o]
            grad = kl_buf[h] + dot_nt(v_ref[:, c], state)
            kg_ref[:, c] = (grad * slope(k_ref[:, c].astype(F32))).astype(BF16)
            vg_ref[:, c] = (vl_buf[h] + dot_nn(kf_buf[h], state)).astype(BF16)

        heads(one)

    last = chunks - 1
    states(0)
    pl.semaphore_wait(barrier, len(everyone))
    exchange(s_out.at[0], s_in.at[0], 0, 0)
    for j in range(1, chunks):
        states(j)
        exchange(s_out.at[0], s_in.at[0], 0, j)
    for j in range(chunks):
        before(j)
    for step in range(chunks + 3):
        if step < chunks:
            group_sum(0, step)
        if 0 <= step - 1 < chunks:
            chip_sum(0, step - 1)
        if 0 <= step - 2 < chunks:
            row_sum(0, step - 2)
        if 0 <= step - 3 < chunks:
            hand_back(0, step - 3)
    for j in range(chunks):
        middle(j)
        if j < last:
            after(j)
    for step in range(chunks + 3):
        if step < chunks:
            group_sum(1, step)
        if step == 0:
            after(last)
        if 0 <= step - 1 < chunks:
            chip_sum(1, step - 1)
        if 0 <= step - 2 < chunks:
            row_sum(1, step - 2)
        if 0 <= step - 3 < chunks:
            hand_back(1, step - 3)
    for j in range(chunks):
        finish(j)

    for way in range(2):
        for j in range(chunks):
            wait_in(s_in.at[way, j], send_a.at[2 * way, j], nz - 1)
            wait_in(p_in.at[way, j], send_a.at[2 * way + 1, j], nz - 1)
            pltpu.make_async_copy(g_in.at[way, j], g_in.at[way, j], send_g.at[way, j]).wait()
            wait_in(t_in.at[way, j], send_t.at[way, j], nx - 1)
            wait_in(u_in.at[way, j], send_u.at[way, j], ny - 1)


def shards(ny, nx, queries, key_vectors, value_vectors, out_grad, doc_ids):
    nz = lax.axis_size("head")
    tokens, features = queries.shape
    count = features // HD
    chunks = count // nz
    vmem = pl.BlockSpec(memory_space=pltpu.VMEM)
    half = functools.partial(pltpu.VMEM, dtype=BF16)
    wide = functools.partial(pltpu.VMEM, dtype=F32)
    dma = pltpu.SemaphoreType.DMA
    message = (HD + TAG, HD)
    out = jax.ShapeDtypeStruct((tokens, features), BF16)
    return pl.pallas_call(
        functools.partial(kernel, ny, nx, nz, chunks),
        out_shape=(out,) * 4,
        in_specs=[pl.BlockSpec(memory_space=pltpu.SMEM)] + [vmem] * 4,
        out_specs=(vmem,) * 4,
        scratch_shapes=[
            half((count, HD, HD)),
            half((count, HD, HD)),
            half((count, HD, HD)),
            half((count, HD, HD)),
            wide((count, HD, HD)),
            wide((count, HD, HD)),
            half((2, chunks, nz, HD, HD)),
            half((2, chunks, nz, HD, HD)),
            half((2, chunks, nz, HD, HD)),
            half((2, chunks, nz, HD, HD)),
            half((2, chunks, *message)),
            half((2, chunks, *message)),
            half((2, chunks, *message)),
            half((2, chunks, nx - 1, *message)),
            half((2, chunks, *message)),
            half((2, chunks, ny - 1, *message)),
            dma((4, chunks)),
            dma((4, chunks)),
            dma((2, chunks)),
            dma((2, chunks)),
            dma((2, chunks)),
            dma((2, chunks)),
            dma((2, chunks)),
            dma((2, chunks)),
        ],
        compiler_params=pltpu.CompilerParams(
            collective_id=0, has_side_effects=True, vmem_limit_bytes=48 * 2**20
        ),
    )(doc_ids, queries, key_vectors, value_vectors, out_grad)


def build(mesh, ny, nx):
    spec = P(("ctx", "head"), None)
    return jax.shard_map(
        functools.partial(shards, ny, nx),
        mesh=mesh,
        in_specs=(spec,) * 4 + (P("ctx"),),
        out_specs=(spec,) * 4,
        check_vma=False,
    )


def solution(mesh):
    return build(mesh, 4, 4)
```

time: 569 us -> 116 us (0.20)
  blocking collectives: 131 us -> 0 us
  Pallas kernels: 0 us -> 108 us
  waiting for transfers between devices: 96.9 us -> 0 us
  loops' own time: 82.7 us -> 0 us
  other arithmetic: 72.6 us -> 0 us
  local copies, waits for them, and re-layouts: 77.4 us -> 5.75 us
  starting transfers between devices: 51 us -> 0 us
  matrix products: 37.9 us -> 0 us
  between operations: 15.1 us -> 0.65 us
    unnamed x2 -> x0, blocking collectives: 131 us -> none
    pallas_call x0 -> x1, Pallas kernels: none -> 108 us  [shards(): pl.pallas_call(functools.partial(kernel, ny, nx, nz, chunks), out_shape=(...]
    all_to_all x8 -> x0, waiting for transfers between devices: 96.8 us -> none  [the longest x1 25.9 us: shards(): lax.all_to_all(grouped(key_vectors), 'head', split_axis=1, concat_axis=0,...]
    another operation x2 -> x0, loops' own time: 82.7 us -> none  [the longest x1 41.4 us: prefix_3(): return lax.fori_loop(0, ahead, one, state)]
    all_to_all x8 -> x0, starting transfers between devices: 51 us -> none  [the longest x1 8.57 us: shards(): lax.all_to_all(grouped(value_vectors), 'head', split_axis=1, concat_axis=...]
    dot_general x20 -> x0, matrix products: 37.9 us -> none  [the longest x4 12.1 us: exact(): return jnp.einsum(form, left, right, precision=lax.Precision.HIGHEST)]
    dynamic_slice x62 -> x0, local copies, waits for them, and re-layouts: 36.4 us -> none  [the longest x31 18.2 us: one(): lax.dynamic_index_in_dim(a, source, 0, False).astype(own.dtype)]
    select_n x31 -> x0, other arithmetic: 32.2 us -> none  [lap(): jnp.where(position < mine, new, old)]
  transfers between devices with their start and end apart: 10 -> 0, of which waited for: 5 -> 0; matrix products, arithmetic and copies ran while one was open for 28% -> 0% of each run, Pallas kernels for 0% -> 0%
where the time goes in v1:
time: 116 us; the launch traced here: 115 us
  Pallas kernels  108 us (93%)
  local copies, waits for them, and re-layouts  5.75 us (5%)
    pallas_call x1, Pallas kernels, shards(): pl.pallas_call(functools.partial(kernel, ny, nx, nz, chunks), out_shape=(...  108 us
    unnamed x8, local copies, waits for them, and re-layouts  5.75 us

profile of v1, /device:TPU:32, one launch (start us, length us, event | category | flops | bytes accessed | tf_op | source)
XLA Modules:
  0.0 114.5 jit_solution(17194470340271973477)
XLA Ops:
  0.6 0.0 copy-start
  0.6 1.2 %copy-done = bf16[128,4096]{1,0:T(8,128)(2,1)S(1)} copy-done((bf16[128,4096]{1,0:T(8,128)(2,1)S(1)}, bf16[128,4096]{1,0:T(8,128)(2,1)}, u32[]{:S(2)}) %copy-start) | copy-done | bytes 1048600
  1.9 0.0 copy-start.1
  1.9 0.7 copy-done.1
  2.5 108.1 %shard_map.84 = (bf16[128,4096]{1,0:T(8,128)(2,1)S(1)}, bf16[128,4096]{1,0:T(8,128)(2,1)S(1)}, bf16[128,4096]{1,0:T(8,128)(2,1)S(1)}, bf16[128,4096]{1,0:T(8,128)(2,1)S(1)}) custom-call(s32[8]{0:T(128)S(1)} %copy-done.1, bf16[128,4096]{1,0:T(8,128)(2,1)S(1)} %copy-done, bf16[128,4096]{1,0:T(8,128)(2,1)} %k_ref.1, bf16[128,4096]{1,0:T(8,128)(2,1)} %v_ref.1, ...), custom_call_target="tpu_custom_call" | custom-call | tf_op jit(solution)/shard_map/pallas_call | solution.py:349
  110.6 1.0 copy.13
  111.6 1.0 copy.14
  112.6 1.0 copy.15
  113.5 1.0 copy.16
Async XLA Ops:
  0.6 1.2 %copy-start = (bf16[128,4096]{1,0:T(8,128)(2,1)S(1)}, bf16[128,4096]{1,0:T(8,128)(2,1)}, u32[]{:S(2)}) copy-start(bf16[128,4096]{1,0:T(8,128)(2,1)} %q_ref.1) | copy-start | bytes 3145732
  1.9 0.7 copy-start.1

commit v2 on v1

v2 whole, which is shorter than its diff:
```python
import functools

import jax
import jax.numpy as jnp
from jax import lax
from jax.experimental import pallas as pl
from jax.experimental.pallas import tpu as pltpu
from jax.sharding import PartitionSpec as P

HD = 128
TAG = 16
MESH = pl.DeviceIdType.MESH
F32 = jnp.float32
BF16 = jnp.bfloat16


def feature(x):
    return jnp.where(x > 0, x + 1.0, jnp.exp(jnp.minimum(x, 0.0)))


def slope(x):
    return jnp.where(x > 0, jnp.ones_like(x), jnp.exp(jnp.minimum(x, 0.0)))


def dot_nn(a, b):
    return lax.dot_general(a, b, (((1,), (0,)), ((), ())), preferred_element_type=F32)


def dot_nt(a, b):
    return lax.dot_general(a, b, (((1,), (1,)), ((), ())), preferred_element_type=F32)


def dot_tn(a, b):
    return lax.dot_general(a, b, (((0,), (0,)), ((), ())), preferred_element_type=F32)


def plan(chunks):
    if chunks == 4:
        order = [
            "S0 T0 B0 S1",
            "T1 B1 S2 C0",
            "T2 C1 B2 S3",
            "G0 T3 C2 X0",
            "G1 X1 Y0 C3",
            "G2 X2 Y1 H0",
            "B3 G3 Y2 X3",
            "H1 E0 Y3 H2",
            "E1 H3 N0 M0",
            "N1 E2 N2 E3",
            "c0 M2 A2 M1",
            "M3 g0 x0 c2",
            "c1 y0 N3 c3",
            "g2 x2 h0 g1",
            "x1 g3 y2 x3",
            "e0 y1 A3 h2",
            "y3 h1 h3 A0",
            "F0 e2 O2 e1",
            "e3 A1 F2 O0",
            "O3 F1 O1 F3",
        ]
        return " ".join(order).split()
    return [f"{step}{j}" for step in "STBCGXYHENMAcgxyheOF" for j in range(chunks)]


def kernel(
    ny,
    nx,
    nz,
    chunks,
    ids,
    q_hbm,
    k_hbm,
    v_hbm,
    g_hbm,
    att_ref,
    qg_ref,
    kg_ref,
    vg_ref,
    q_ref,
    k_ref,
    v_ref,
    g_ref,
    load_sem,
    kf_buf,
    qf_buf,
    a_buf,
    sc_buf,
    kl_buf,
    vl_buf,
    s_out,
    leaf_in,
    up_out,
    up_in,
    p_out,
    p_in,
    aux_in,
    ex_out,
    g_out,
    g_in,
    t_out,
    t_in,
    u_out,
    u_in,
    send_a,
    recv_a,
    send_more,
    recv_more,
    send_g,
    recv_g,
    send_t,
    recv_t,
    send_u,
    recv_u,
):
    ctx = lax.axis_index("ctx")
    z = lax.axis_index("head")
    core = lax.rem(ctx, 2)
    x = lax.rem(ctx // 2, nx)
    y = ctx // (2 * nx)

    def at(yy, xx, cc):
        return (yy * nx + xx) * 2 + cc

    peer = (at(y, x, 1 - core), z)
    lines = [(ctx, lax.rem(z + d, nz)) for d in (1, 2, nz - 1, nz - 2)]
    rows = [(at(y, lax.rem(x + d, nx), core), z) for d in range(1, nx)]
    columns = [(at(lax.rem(y + d, ny), x, core), z) for d in range(1, ny)]
    everyone = lines + rows + columns + [peer]

    barrier = pltpu.get_barrier_semaphore()
    for device in everyone:
        pl.semaphore_signal(barrier, inc=1, device_id=device, device_id_type=MESH)

    def block(ref, j):
        return ref.at[:, pl.ds(j * nz * HD, nz * HD)]

    def load(i, j):
        hbm, ref = ((k_hbm, k_ref), (v_hbm, v_ref), (q_hbm, q_ref), (g_hbm, g_ref))[i]
        return pltpu.make_async_copy(block(hbm, j), block(ref, j), load_sem.at[i, j])

    for i in range(0, 4, 2):
        for j in range(chunks):
            load(i, j).start()
            load(i + 1, j).start()

    core_one = (core == 1).astype(F32)
    doc = [ids[i] for i in range(nz)]
    causal = lax.broadcasted_iota(jnp.int32, (HD, HD), 0) >= lax.broadcasted_iota(
        jnp.int32, (HD, HD), 1
    )

    def alike(a, b):
        return jnp.where(a == b, 1.0, 0.0).astype(F32)

    def place(way):
        return z if way == 0 else nz - 1 - z

    def line(way, v):
        v = lax.rem(v + 2 * nz, nz)
        return (ctx, v if way == 0 else nz - 1 - v)

    def doc_at(way, v):
        v = lax.rem(v + 2 * nz, nz)
        return ids[v if way == 0 else nz - 1 - v]

    def following(way, v):
        return doc_at(way, jnp.minimum(v + 1, nz - 1))

    def slot(v):
        return lax.rem(v + 2 * nz, nz)

    def head_slot(way, o):
        return o if way == 0 else nz - 1 - o

    def columns_of(h):
        return pl.ds(pl.multiple_of(h * HD, HD), HD)

    def remote(src, dst, send, recv, device):
        return pltpu.make_async_remote_copy(
            src_ref=src,
            dst_ref=dst,
            send_sem=send,
            recv_sem=recv,
            device_id=device,
            device_id_type=MESH,
        )

    def wait_in(into, sem, count):
        part = into.at[pl.ds(0, count)]
        pltpu.make_async_copy(part, part, sem).wait()

    def near(body):
        for off in (0, 1, 2, nz - 2, nz - 1):
            body(lax.rem(z + off, nz))

    def far(body):
        for off in range(3, nz - 2):
            body(lax.rem(z + off, nz))

    def every(body):
        for o in range(nz):
            body(o)

    def states(j, some):
        def one(o):
            h = nz * j + o
            c = columns_of(h)
            kf = feature(k_ref[:, c].astype(F32)).astype(BF16)
            kf_buf[h] = kf
            s_out[0, j, o] = dot_tn(kf, v_ref[:, c]).astype(BF16)

        some(one)

    def before(j):
        load(2, j).wait()
        load(3, j).wait()

        def one(o):
            h = nz * j + o
            c = columns_of(h)
            qf = feature(q_ref[:, c].astype(F32)).astype(BF16)
            qf_buf[h] = qf
            a_buf[h] = jnp.where(causal, dot_nt(qf, kf_buf[h]), 0.0).astype(BF16)

        every(one)

    averaging = jnp.full((HD, HD), 1.0 / HD, BF16)

    def row_mean(product):
        return dot_nn(product.astype(BF16), averaging)

    def tag_of(message):
        return message[pl.ds(HD, TAG), :].astype(F32)[0:1, :]

    def value_of(message):
        return message[pl.ds(0, HD), :].astype(F32)

    def put(message, value, tag):
        message[pl.ds(0, HD), :] = value.astype(BF16)
        message[pl.ds(HD, TAG), :] = jnp.broadcast_to(tag, (TAG, HD)).astype(BF16)

    def send_to(src, dst, way, phase, j, device):
        remote(src, dst, send_a.at[way, phase, j], recv_a.at[way, phase, j], device).start()

    def send_more_to(src, dst, way, phase, j, device):
        remote(
            src, dst, send_more.at[way, phase, j], recv_more.at[way, phase, j], device
        ).start()

    def one_more(way, phase, j, sem):
        part = aux_in.at[way, j, 0]
        pltpu.make_async_copy(part, part, sem.at[way, phase, j]).wait()

    def spread(way, j):
        v = place(way)
        source = s_out.at[way, j]
        into = leaf_in.at[way, j]
        send_to(source.at[slot(v - 4)], into.at[1], way, 0, j, line(way, v - 2))
        send_to(source.at[slot(v - 3)], into.at[0], way, 0, j, line(way, v - 1))
        send_to(source.at[slot(v + 3)], into.at[2], way, 0, j, line(way, v + 1))

    def collect(way, j):
        v = place(way)
        alone = alike(doc_at(way, v), following(way, v))
        mine, up, into = s_out.at[way, j], up_out.at[way, j], up_in.at[way, j]

        def state(u):
            return mine[slot(u)].astype(F32)

        up[0] = (alone * state(v - 1)).astype(BF16)
        up[1] = (alone * state(v + 1)).astype(BF16)
        into[v] = (alone * state(v)).astype(BF16)
        send_to(up.at[0], into.at[v], way, 1, j, line(way, v - 1))
        send_to(up.at[1], into.at[v], way, 1, j, line(way, v + 1))
        wait_in(leaf_in.at[way, j], recv_a.at[way, 0, j], 3)
        first, second, behind = (leaf_in[way, j, i].astype(F32) for i in range(3))
        after_run = following(way, jnp.minimum(v + 2, nz - 1))

        def weight(inside, u, target):
            return inside.astype(F32) * alike(doc_at(way, u), target)

        up[2] = (
            alike(doc_at(way, v), after_run) * state(v - 2)
            + weight(v + 1 < nz, v + 1, after_run) * first
            + weight(v + 2 < nz, v + 2, after_run) * second
        ).astype(BF16)
        send_to(up.at[2], into.at[v], way, 1, j, line(way, v - 2))
        up[3] = (
            alone * state(v + 2) + weight(v > 0, v - 1, following(way, v)) * behind
        ).astype(BF16)
        send_to(up.at[3], into.at[jnp.maximum(v - 1, 0)], way, 1, j, line(way, v + 2))

        @pl.when(v >= nz - 2)
        def _():
            target = doc_at(way, v + 3)
            up[4] = (
                weight(v + 1 >= nz, v + 1, target) * first
                + weight(v + 2 >= nz, v + 2, target) * second
            ).astype(BF16)
            send_more_to(up.at[4], into.at[0], way, 0, j, line(way, v - 2))

        @pl.when(v == 0)
        def _():
            up[4] = leaf_in[way, j, 2]
            send_more_to(up.at[4], into.at[nz - 1], way, 0, j, line(way, v + 2))

    def segments(way):
        v = place(way)
        result = []
        for i in range(nz):
            off = lax.rem(i - v + nz, nz)
            length = jnp.where(off == 2, 3, jnp.where(off == 5, 2, 1))
            inner = (off == 3) | (off == 4) | (off == 6)
            if i == 0:
                length = jnp.where(off == 3, 2, length)
                start = None
                keep = alike(doc_at(way, i), following(way, i + length - 1))
            else:
                start = jnp.logical_not(inner)
                end = jnp.minimum(i + length - 1, nz - 1)
                keep = jnp.where(inner, 1.0, alike(doc_at(way, i), following(way, end)))
            result.append((start, keep))
        return result

    def part_of(way, j, i, start):
        value = up_in[way, j, i].astype(F32)
        return value if start is None else jnp.where(start, value, 0.0)

    def group_sum(way, j):
        v = place(way)
        wait_in(up_in.at[way, j], recv_a.at[way, 1, j], 4)

        @pl.when((v == 2) | (v == 4) | (v == 5))
        def _():
            one_more(way, 0, j, recv_more)

        total = jnp.zeros((HD, HD), F32)
        for i, (start, keep) in enumerate(segments(way)):
            total = keep * total + part_of(way, j, i, start)
        edge = doc_at(way, nz - 1)
        put(g_out.at[way, j], total, edge.astype(F32) * jnp.ones((1, HD), F32))
        remote(
            g_out.at[way, j], g_in.at[way, j], send_g.at[way, j], recv_g.at[way, j], peer
        ).start()

    def chip_sum(way, j):
        pltpu.make_async_copy(g_in.at[way, j], g_in.at[way, j], recv_g.at[way, j]).wait()
        mine, other = g_out.at[way, j], g_in.at[way, j]
        late = core_one if way == 0 else 1.0 - core_one
        same = alike(tag_of(mine), tag_of(other))
        keep_mine = late + (1.0 - late) * same
        keep_other = (1.0 - late) + late * same
        put(
            t_out.at[way, j],
            keep_mine * value_of(mine) + keep_other * value_of(other),
            late * tag_of(mine) + (1.0 - late) * tag_of(other),
        )
        for d, device in enumerate(rows):
            remote(
                t_out.at[way, j],
                t_in.at[way, j, d],
                send_t.at[way, j],
                recv_t.at[way, j],
                device,
            ).start()

    def row_sum(way, j):
        if nx > 1:
            wait_in(t_in.at[way, j], recv_t.at[way, j], nx - 1)
        edge = nx - 1 if way == 0 else 0
        parts = [(t_out.at[way, j], x)] + [
            (t_in.at[way, j, d], lax.rem(x + nx - 1 - d, nx)) for d in range(nx - 1)
        ]
        tag = jnp.zeros((1, HD), F32)
        for part, place in parts:
            tag = tag + alike(place, edge) * tag_of(part)
        total = jnp.zeros((HD, HD), F32)
        for part, place in parts:
            total = total + alike(tag_of(part), tag) * value_of(part)
        put(u_out.at[way, j], total, tag)
        for d, device in enumerate(columns):
            remote(
                u_out.at[way, j],
                u_in.at[way, j, d],
                send_u.at[way, j],
                recv_u.at[way, j],
                device,
            ).start()

    def hand_back(way, j):
        if ny > 1:
            wait_in(u_in.at[way, j], recv_u.at[way, j], ny - 1)
        want = (doc[0] if way == 0 else doc[nz - 1]).astype(F32)
        late = core_one if way == 0 else 1.0 - core_one
        other = g_in.at[way, j]
        running = late * alike(tag_of(other), want) * value_of(other)
        for d in range(nx - 1):
            before_me = (x >= d + 1) if way == 0 else (x < d + 1)
            part = t_in.at[way, j, d]
            running = running + before_me.astype(F32) * alike(tag_of(part), want) * value_of(part)
        for d in range(ny - 1):
            before_me = (y >= d + 1) if way == 0 else (y < d + 1)
            part = u_in.at[way, j, d]
            running = running + before_me.astype(F32) * alike(tag_of(part), want) * value_of(part)
        v = place(way)
        for i, (start, keep) in enumerate(segments(way)):
            p_out[way, j, i] = running.astype(BF16)
            if i < nz - 1:
                running = keep * running + part_of(way, j, i, start)
        out, into, aux = p_out.at[way, j], p_in.at[way, j], aux_in.at[way, j]
        behind = jnp.where(slot(v - 2) == 0, 0, slot(v - 3))
        send_to(out.at[behind], aux.at[0], way, 2, j, line(way, v - 2))
        send_to(out.at[slot(v + 2)], into.at[v], way, 2, j, line(way, v + 2))

        @pl.when((v == 4) | (v == 5))
        def _():
            send_more_to(out.at[0], aux.at[1], way, 1, j, line(way, v + 2))

        @pl.when(v == 2)
        def _():
            send_more_to(out.at[nz - 1], aux.at[1], way, 1, j, line(way, v - 2))

        send_to(out.at[slot(v - 1)], into.at[v], way, 2, j, line(way, v - 1))
        send_to(out.at[slot(v + 1)], into.at[v], way, 2, j, line(way, v + 1))
        p_in[way, j, v] = p_out[way, j, v]

    def expand(way, j):
        v = place(way)
        wait_in(p_in.at[way, j], recv_a.at[way, 2, j], 4)
        more = (v >= nz - 2) | (v == 0)

        @pl.when(more)
        def _():
            one_more(way, 1, j, recv_more)

        mine, leaf, aux, out = s_out.at[way, j], leaf_in.at[way, j], aux_in.at[way, j], ex_out.at[way, j]

        def step(u, value, state):
            return alike(doc_at(way, u), doc_at(way, u + 1)) * (value + state.astype(F32))

        extra = jnp.where(more, aux[1].astype(F32), 0.0)
        here = p_in[way, j, slot(v - 2)].astype(F32)
        one = jnp.where(v + 1 == nz, extra, step(v, here, mine[slot(v - 2)]))
        two = jnp.where(v + 2 == nz, extra, step(v + 1, one, leaf[0]))
        out[1] = two.astype(BF16)
        send_to(out.at[1], p_in.at[way, j, slot(v - 2)], way, 3, j, line(way, v + 2))
        out[0] = one.astype(BF16)
        send_to(out.at[0], p_in.at[way, j, slot(v - 2)], way, 3, j, line(way, v + 1))
        begin = aux[0].astype(F32)
        out[2] = jnp.where(v == 0, extra, begin).astype(BF16)
        send_to(out.at[2], p_in.at[way, j, slot(v + 2)], way, 3, j, line(way, v - 1))
        own = jnp.where(v == 0, begin, step(v - 1, begin, leaf[2]))
        p_in[way, j, slot(v + 2)] = own.astype(BF16)

    def middle(j, some):
        def one(o):
            h = nz * j + o
            c = columns_of(h)
            qf = qf_buf[h]
            raw = dot_nn(a_buf[h], v_ref[:, c]) + dot_nn(qf, p_in[0, j, o])
            inverse = lax.rsqrt(row_mean(raw * raw) + 1e-06)
            normed = raw * inverse
            att_ref[:, c] = normed.astype(BF16)
            wide = g_ref[:, c].astype(F32)
            along = row_mean(wide * normed)
            scaled = ((wide - normed * along) * inverse).astype(BF16)
            sc_buf[h] = scaled
            s_out[1, j, nz - 1 - o] = dot_tn(qf, scaled).astype(BF16)

        some(one)

    def middle_far(j):
        wait_in(p_in.at[0, j], recv_a.at[0, 3, j], 3)
        middle(j, far)
        spread(1, j)

    def after(j):
        def one(o):
            h = nz * j + o
            c = columns_of(h)
            scaled = sc_buf[h]
            mixed = jnp.where(causal, dot_nt(scaled, v_ref[:, c]), 0.0).astype(BF16)
            grad = dot_nn(mixed, kf_buf[h]) + dot_nt(scaled, p_in[0, j, o])
            qg_ref[:, c] = (grad * slope(q_ref[:, c].astype(F32))).astype(BF16)
            kl_buf[h] = dot_tn(mixed, qf_buf[h])
            vl_buf[h] = dot_tn(a_buf[h], scaled)

        every(one)

    def finish(j, some):
        def one(o):
            h = nz * j + o
            c = columns_of(h)
            state = p_in[1, j, nz - 1 - o]
            grad = kl_buf[h] + dot_nt(v_ref[:, c], state)
            kg_ref[:, c] = (grad * slope(k_ref[:, c].astype(F32))).astype(BF16)
            vg_ref[:, c] = (vl_buf[h] + dot_nn(kf_buf[h], state)).astype(BF16)

        some(one)

    def finish_far(j):
        wait_in(p_in.at[1, j], recv_a.at[1, 3, j], 3)
        finish(j, far)

    def start_states(j):
        load(0, j).wait()
        load(1, j).wait()
        states(j, far)
        if j == 0:
            pl.semaphore_wait(barrier, len(everyone))
        spread(0, j)

    steps = {
        "S": start_states,
        "B": before,
        "T": lambda j: states(j, near),
        "N": lambda j: middle(j, near),
        "M": middle_far,
        "A": after,
        "O": lambda j: finish(j, near),
        "F": finish_far,
        "C": functools.partial(collect, 0),
        "E": functools.partial(expand, 0),
        "c": functools.partial(collect, 1),
        "e": functools.partial(expand, 1),
        "G": functools.partial(group_sum, 0),
        "X": functools.partial(chip_sum, 0),
        "Y": functools.partial(row_sum, 0),
        "H": functools.partial(hand_back, 0),
        "g": functools.partial(group_sum, 1),
        "x": functools.partial(chip_sum, 1),
        "y": functools.partial(row_sum, 1),
        "h": functools.partial(hand_back, 1),
    }
    for step in plan(chunks):
        steps[step[0]](int(step[1:]))

    for way in range(2):
        v = place(way)
        for j in range(chunks):
            for phase, count in enumerate((3, 4, 4, 3)):
                wait_in(p_in.at[way, j], send_a.at[way, phase, j], count)
            pltpu.make_async_copy(g_in.at[way, j], g_in.at[way, j], send_g.at[way, j]).wait()
            if nx > 1:
                wait_in(t_in.at[way, j], send_t.at[way, j], nx - 1)
            if ny > 1:
                wait_in(u_in.at[way, j], send_u.at[way, j], ny - 1)

            @pl.when((v >= nz - 2) | (v == 0))
            def _():
                one_more(way, 0, j, send_more)

            @pl.when((v == 2) | (v == 4) | (v == 5))
            def _():
                one_more(way, 1, j, send_more)


def shards(ny, nx, queries, key_vectors, value_vectors, out_grad, doc_ids):
    nz = lax.axis_size("head")
    tokens, features = queries.shape
    count = features // HD
    chunks = count // nz
    anywhere = pl.BlockSpec(memory_space=pl.ANY)
    half = functools.partial(pltpu.VMEM, dtype=BF16)
    wide = functools.partial(pltpu.VMEM, dtype=F32)
    dma = pltpu.SemaphoreType.DMA
    message = (HD + TAG, HD)
    out = pltpu.VMEM((tokens, features), BF16)
    return pl.pallas_call(
        functools.partial(kernel, ny, nx, nz, chunks),
        out_shape=(out,) * 4,
        in_specs=[pl.BlockSpec(memory_space=pltpu.SMEM)] + [anywhere] * 4,
        out_specs=(pl.BlockSpec(memory_space=pltpu.VMEM),) * 4,
        scratch_shapes=[half((tokens, features))] * 4
        + [dma((4, chunks))]
        + [
            half((count, HD, HD)),
            half((count, HD, HD)),
            half((count, HD, HD)),
            half((count, HD, HD)),
            wide((count, HD, HD)),
            wide((count, HD, HD)),
            half((2, chunks, nz, HD, HD)),
            half((2, chunks, 3, HD, HD)),
            half((2, chunks, 5, HD, HD)),
            half((2, chunks, nz, HD, HD)),
            half((2, chunks, nz, HD, HD)),
            half((2, chunks, nz, HD, HD)),
            half((2, chunks, 2, HD, HD)),
            half((2, chunks, 3, HD, HD)),
            half((2, chunks, *message)),
            half((2, chunks, *message)),
            half((2, chunks, *message)),
            half((2, chunks, max(nx - 1, 1), *message)),
            half((2, chunks, *message)),
            half((2, chunks, max(ny - 1, 1), *message)),
            dma((2, 4, chunks)),
            dma((2, 4, chunks)),
            dma((2, 2, chunks)),
            dma((2, 2, chunks)),
            dma((2, chunks)),
            dma((2, chunks)),
            dma((2, chunks)),
            dma((2, chunks)),
            dma((2, chunks)),
            dma((2, chunks)),
        ],
        compiler_params=pltpu.CompilerParams(
            collective_id=0, has_side_effects=True, vmem_limit_bytes=56 * 2**20
        ),
    )(doc_ids, queries, key_vectors, value_vectors, out_grad)


def build(mesh, ny, nx):
    spec = P(("ctx", "head"), None)
    return jax.shard_map(
        functools.partial(shards, ny, nx),
        mesh=mesh,
        in_specs=(spec,) * 4 + (P("ctx"),),
        out_specs=(spec,) * 4,
        check_vma=False,
    )


def solution(mesh):
    return build(mesh, 4, 4)
```

time: 116 us -> 102 us (0.88)
  Pallas kernels: 108 us -> 96.8 us
  local copies, waits for them, and re-layouts: 5.75 us -> 3.88 us
    pallas_call x1, Pallas kernels: 108 us -> 96.8 us  [shards(): pl.pallas_call(functools.partial(kernel, ny, nx, nz, chunks), out_shape=(...]
    unnamed x8 -> x4, local copies, waits for them, and re-layouts: 5.75 us -> 3.88 us
where the time goes in v2:
time: 102 us; the launch traced here: 101 us
  Pallas kernels  96.8 us (95%)
  local copies, waits for them, and re-layouts  3.88 us (4%)
    pallas_call x1, Pallas kernels, shards(): pl.pallas_call(functools.partial(kernel, ny, nx, nz, chunks), out_shape=(...  96.8 us
    unnamed x4, local copies, waits for them, and re-layouts  3.88 us

profile of v2, /device:TPU:32, one launch (start us, length us, event | category | flops | bytes accessed | tf_op | source)
XLA Modules:
  0.0 101.3 jit_solution(16533089865038505911)
XLA Ops:
  0.6 96.8 %shard_map.84 = (bf16[128,4096]{1,0:T(8,128)(2,1)S(1)}, bf16[128,4096]{1,0:T(8,128)(2,1)S(1)}, bf16[128,4096]{1,0:T(8,128)(2,1)S(1)}, bf16[128,4096]{1,0:T(8,128)(2,1)S(1)}) custom-call(s32[8]{0:T(128)} %ids.1, bf16[128,4096]{1,0:T(8,128)(2,1)} %q_hbm.1, bf16[128,4096]{1,0:T(8,128)(2,1)} %k_hbm.1, bf16[128,4096]{1,0:T(8,128)(2,1)} %v_hbm.1, ...), custom_call_target="tpu_custom_call" | custom-call | tf_op jit(solution)/shard_map/pallas_call | solution.py:569
  97.4 1.0 copy.13
  98.4 1.0 copy.14
  99.4 1.0 copy.15
  100.3 1.0 copy.16

commit v3 on v2

--- a/solution.py
+++ b/solution.py
@@ -37,26 +37,26 @@
 def plan(chunks):
     if chunks == 4:
         order = [
-            "S0 T0 B0 S1",
-            "T1 B1 S2 C0",
-            "T2 C1 B2 S3",
-            "G0 T3 C2 X0",
-            "G1 X1 Y0 C3",
-            "G2 X2 Y1 H0",
-            "B3 G3 Y2 X3",
-            "H1 E0 Y3 H2",
-            "E1 H3 N0 M0",
-            "N1 E2 N2 E3",
-            "c0 M2 A2 M1",
-            "M3 g0 x0 c2",
-            "c1 y0 N3 c3",
-            "g2 x2 h0 g1",
-            "x1 g3 y2 x3",
-            "e0 y1 A3 h2",
-            "y3 h1 h3 A0",
-            "F0 e2 O2 e1",
-            "e3 A1 F2 O0",
-            "O3 F1 O1 F3",
+            "S0 S3 T3 T0",
+            "B0 S1 T1 S2",
+            "C3 C1 T2 B3",
+            "B2 C0 G3 B1",
+            "C2 X3 G1 X1",
+            "G0 Y3 X0 G2",
+            "Y1 X2 H3 Y0",
+            "H1 Y2 H0 H2",
+            "E1 E0 N0 E3",
+            "E2 M1 M0 N1",
+            "M3 M2 N2 c1",
+            "N3 c0 A0 A1",
+            "c3 g1 x1 c2",
+            "g0 A2 x0 g3",
+            "y1 x3 g2 y0",
+            "x2 y3 h1 h0",
+            "y2 h3 h2 e0",
+            "O0 e1 O1 e3",
+            "A3 e2 O2 F1",
+            "F0 O3 F3 F2",
         ]
         return " ".join(order).split()
     return [f"{step}{j}" for step in "STBCGXYHENMAcgxyheOF" for j in range(chunks)]
@@ -251,11 +251,21 @@
         part = aux_in.at[way, j, 0]
         pltpu.make_async_copy(part, part, sem.at[way, phase, j]).wait()
 
+    def leans(j):
+        return j % 2 == 1
+
+    def split_at(j, v):
+        return (v == nz - 1) | (v <= 1) if leans(j) else (v >= nz - 2) | (v == 0)
+
+    def split_for(j, v):
+        return (v == 2) | (v == 3) | (v == 5) if leans(j) else (v == 2) | (v == 4) | (v == 5)
+
     def spread(way, j):
         v = place(way)
         source = s_out.at[way, j]
         into = leaf_in.at[way, j]
-        send_to(source.at[slot(v - 4)], into.at[1], way, 0, j, line(way, v - 2))
+        beyond = line(way, v + 2 if leans(j) else v - 2)
+        send_to(source.at[slot(v - 4)], into.at[1], way, 0, j, beyond)
         send_to(source.at[slot(v - 3)], into.at[0], way, 0, j, line(way, v - 1))
         send_to(source.at[slot(v + 3)], into.at[2], way, 0, j, line(way, v + 1))
 
@@ -274,45 +284,59 @@
         send_to(up.at[1], into.at[v], way, 1, j, line(way, v + 1))
         wait_in(leaf_in.at[way, j], recv_a.at[way, 0, j], 3)
         first, second, behind = (leaf_in[way, j, i].astype(F32) for i in range(3))
-        after_run = following(way, jnp.minimum(v + 2, nz - 1))
+        ahead, back = (1, 2) if leans(j) else (2, 1)
+        after_run = following(way, jnp.minimum(v + ahead, nz - 1))
 
         def weight(inside, u, target):
             return inside.astype(F32) * alike(doc_at(way, u), target)
 
-        up[2] = (
+        forward = (
             alike(doc_at(way, v), after_run) * state(v - 2)
             + weight(v + 1 < nz, v + 1, after_run) * first
-            + weight(v + 2 < nz, v + 2, after_run) * second
-        ).astype(BF16)
+        )
+        if not leans(j):
+            forward = forward + weight(v + 2 < nz, v + 2, after_run) * second
+        up[2] = forward.astype(BF16)
         send_to(up.at[2], into.at[v], way, 1, j, line(way, v - 2))
-        up[3] = (
-            alone * state(v + 2) + weight(v > 0, v - 1, following(way, v)) * behind
-        ).astype(BF16)
-        send_to(up.at[3], into.at[jnp.maximum(v - 1, 0)], way, 1, j, line(way, v + 2))
-
-        @pl.when(v >= nz - 2)
+        backward = alone * state(v + 2) + weight(v > 0, v - 1, following(way, v)) * behind
+        if leans(j):
+            backward = backward + weight(v > 1, v - 2, following(way, v)) * second
+        up[3] = backward.astype(BF16)
+        send_to(up.at[3], into.at[jnp.maximum(v - back, 0)], way, 1, j, line(way, v + 2))
+
+        @pl.when(v >= nz - ahead)
         def _():
-            target = doc_at(way, v + 3)
-            up[4] = (
-                weight(v + 1 >= nz, v + 1, target) * first
-                + weight(v + 2 >= nz, v + 2, target) * second
-            ).astype(BF16)
+            target = doc_at(way, v + 1 + ahead)
+            rest = weight(v + 1 >= nz, v + 1, target) * first
+            if not leans(j):
+                rest = rest + weight(v + 2 >= nz, v + 2, target) * second
+            up[4] = rest.astype(BF16)
             send_more_to(up.at[4], into.at[0], way, 0, j, line(way, v - 2))
 
-        @pl.when(v == 0)
+        @pl.when(v < back)
         def _():
-            up[4] = leaf_in[way, j, 2]
-            send_more_to(up.at[4], into.at[nz - 1], way, 0, j, line(way, v + 2))
-
-    def segments(way):
+            target = doc_at(way, nz - 1)
+            rest = weight(v < 1, v - 1, target) * behind
+            if leans(j):
+                rest = rest + weight(v < 2, v - 2, target) * second
+            up[4] = rest.astype(BF16)
+            send_more_to(up.at[4], into.at[slot(v - back)], way, 0, j, line(way, v + 2))
+
+    def segments(way, j):
         v = place(way)
         result = []
         for i in range(nz):
             off = lax.rem(i - v + nz, nz)
-            length = jnp.where(off == 2, 3, jnp.where(off == 5, 2, 1))
-            inner = (off == 3) | (off == 4) | (off == 6)
+            if leans(j):
+                length = jnp.where(off == 2, 2, jnp.where(off == 4, 3, 1))
+                inner = (off == 3) | (off == 5) | (off == 6)
+                cut = 5
+            else:
+                length = jnp.where(off == 2, 3, jnp.where(off == 5, 2, 1))
+                inner = (off == 3) | (off == 4) | (off == 6)
+                cut = 3
             if i == 0:
-                length = jnp.where(off == 3, 2, length)
+                length = jnp.where(off == cut, 2, length)
                 start = None
                 keep = alike(doc_at(way, i), following(way, i + length - 1))
             else:
@@ -330,12 +354,12 @@
         v = place(way)
         wait_in(up_in.at[way, j], recv_a.at[way, 1, j], 4)
 
-        @pl.when((v == 2) | (v == 4) | (v == 5))
+        @pl.when(split_for(j, v))
         def _():
             one_more(way, 0, j, recv_more)
 
         total = jnp.zeros((HD, HD), F32)
-        for i, (start, keep) in enumerate(segments(way)):
+        for i, (start, keep) in enumerate(segments(way, j)):
             total = keep * total + part_of(way, j, i, start)
         edge = doc_at(way, nz - 1)
         put(g_out.at[way, j], total, edge.astype(F32) * jnp.ones((1, HD), F32))
@@ -403,22 +427,24 @@
             part = u_in.at[way, j, d]
             running = running + before_me.astype(F32) * alike(tag_of(part), want) * value_of(part)
         v = place(way)
-        for i, (start, keep) in enumerate(segments(way)):
+        for i, (start, keep) in enumerate(segments(way, j)):
             p_out[way, j, i] = running.astype(BF16)
             if i < nz - 1:
                 running = keep * running + part_of(way, j, i, start)
         out, into, aux = p_out.at[way, j], p_in.at[way, j], aux_in.at[way, j]
-        behind = jnp.where(slot(v - 2) == 0, 0, slot(v - 3))
-        send_to(out.at[behind], aux.at[0], way, 2, j, line(way, v - 2))
+        ahead, back = (1, 2) if leans(j) else (2, 1)
+        behind = slot(v - 2)
+        begin = jnp.maximum(behind - back, 0)
+        send_to(out.at[begin], aux.at[0], way, 2, j, line(way, v - 2))
         send_to(out.at[slot(v + 2)], into.at[v], way, 2, j, line(way, v + 2))
 
-        @pl.when((v == 4) | (v == 5))
+        @pl.when(slot(v + 2) >= nz - ahead)
         def _():
             send_more_to(out.at[0], aux.at[1], way, 1, j, line(way, v + 2))
 
-        @pl.when(v == 2)
+        @pl.when(behind < back)
         def _():
-            send_more_to(out.at[nz - 1], aux.at[1], way, 1, j, line(way, v - 2))
+            send_more_to(out.at[slot(behind - back)], aux.at[1], way, 1, j, line(way, v - 2))
 
         send_to(out.at[slot(v - 1)], into.at[v], way, 2, j, line(way, v - 1))
         send_to(out.at[slot(v + 1)], into.at[v], way, 2, j, line(way, v + 1))
@@ -427,30 +453,38 @@
     def expand(way, j):
         v = place(way)
         wait_in(p_in.at[way, j], recv_a.at[way, 2, j], 4)
-        more = (v >= nz - 2) | (v == 0)
+        more = split_at(j, v)
 
         @pl.when(more)
         def _():
             one_more(way, 1, j, recv_more)
 
-        mine, leaf, aux, out = s_out.at[way, j], leaf_in.at[way, j], aux_in.at[way, j], ex_out.at[way, j]
+        mine, leaf = s_out.at[way, j], leaf_in.at[way, j]
+        aux, out = aux_in.at[way, j], ex_out.at[way, j]
+        ours, theirs = p_in.at[way, j, slot(v - 2)], p_in.at[way, j, slot(v + 2)]
 
         def step(u, value, state):
             return alike(doc_at(way, u), doc_at(way, u + 1)) * (value + state.astype(F32))
 
         extra = jnp.where(more, aux[1].astype(F32), 0.0)
-        here = p_in[way, j, slot(v - 2)].astype(F32)
-        one = jnp.where(v + 1 == nz, extra, step(v, here, mine[slot(v - 2)]))
-        two = jnp.where(v + 2 == nz, extra, step(v + 1, one, leaf[0]))
-        out[1] = two.astype(BF16)
-        send_to(out.at[1], p_in.at[way, j, slot(v - 2)], way, 3, j, line(way, v + 2))
+        begin = aux[0].astype(F32)
+        one = jnp.where(v + 1 == nz, extra, step(v, ours[...].astype(F32), mine[slot(v - 2)]))
+        if leans(j):
+            far_one = jnp.where(v < 2, extra, begin)
+            out[1] = far_one.astype(BF16)
+            send_to(out.at[1], theirs, way, 3, j, line(way, v - 2))
+            last_one = jnp.where(v == 1, begin, step(v - 2, far_one, leaf[1]))
+        else:
+            far_one = jnp.where(v + 2 == nz, extra, step(v + 1, one, leaf[0]))
+            out[1] = far_one.astype(BF16)
+            send_to(out.at[1], ours, way, 3, j, line(way, v + 2))
+            last_one = jnp.where(v == 0, extra, begin)
         out[0] = one.astype(BF16)
-        send_to(out.at[0], p_in.at[way, j, slot(v - 2)], way, 3, j, line(way, v + 1))
-        begin = aux[0].astype(F32)
-        out[2] = jnp.where(v == 0, extra, begin).astype(BF16)
-        send_to(out.at[2], p_in.at[way, j, slot(v + 2)], way, 3, j, line(way, v - 1))
-        own = jnp.where(v == 0, begin, step(v - 1, begin, leaf[2]))
-        p_in[way, j, slot(v + 2)] = own.astype(BF16)
+        send_to(out.at[0], ours, way, 3, j, line(way, v + 1))
+        out[2] = last_one.astype(BF16)
+        send_to(out.at[2], theirs, way, 3, j, line(way, v - 1))
+        here = jnp.where(v == 0, begin, step(v - 1, last_one, leaf[2]))
+        theirs[...] = here.astype(BF16)
 
     def middle(j, some):
         def one(o):
@@ -546,11 +580,11 @@
             if ny > 1:
                 wait_in(u_in.at[way, j], send_u.at[way, j], ny - 1)
 
-            @pl.when((v >= nz - 2) | (v == 0))
+            @pl.when(split_at(j, v))
             def _():
                 one_more(way, 0, j, send_more)
 
-            @pl.when((v == 2) | (v == 4) | (v == 5))
+            @pl.when(split_for(j, v))
             def _():
                 one_more(way, 1, j, send_more)
 

time: 102 us -> 99 us (0.971)
  Pallas kernels: 96.8 us -> 93.8 us
    pallas_call x1, Pallas kernels: 96.8 us -> 93.8 us  [shards(): pl.pallas_call(functools.partial(kernel, ny, nx, nz, chunks), out_shape=(...]
where the time goes in v3:
time: 99 us; the launch traced here: 98.4 us
  Pallas kernels  93.8 us (95%)
  local copies, waits for them, and re-layouts  3.88 us (4%)
    pallas_call x1, Pallas kernels, shards(): pl.pallas_call(functools.partial(kernel, ny, nx, nz, chunks), out_shape=(...  93.8 us
    unnamed x4, local copies, waits for them, and re-layouts  3.88 us

profile of v3, /device:TPU:32, one launch (start us, length us, event | category | flops | bytes accessed | tf_op | source)
XLA Modules:
  0.0 98.4 jit_solution(4490335519198243101)
XLA Ops:
  0.6 93.8 %shard_map.84 = (bf16[128,4096]{1,0:T(8,128)(2,1)S(1)}, bf16[128,4096]{1,0:T(8,128)(2,1)S(1)}, bf16[128,4096]{1,0:T(8,128)(2,1)S(1)}, bf16[128,4096]{1,0:T(8,128)(2,1)S(1)}) custom-call(s32[8]{0:T(128)} %ids.1, bf16[128,4096]{1,0:T(8,128)(2,1)} %q_hbm.1, bf16[128,4096]{1,0:T(8,128)(2,1)} %k_hbm.1, bf16[128,4096]{1,0:T(8,128)(2,1)} %v_hbm.1, ...), custom_call_target="tpu_custom_call" | custom-call | tf_op jit(solution)/shard_map/pallas_call | solution.py:603
  94.5 1.0 copy.13
  95.4 1.0 copy.14
  96.4 1.0 copy.15
  97.4 1.0 copy.16

commit v4 on v3

--- a/solution.py
+++ b/solution.py
@@ -37,26 +37,26 @@
 def plan(chunks):
     if chunks == 4:
         order = [
-            "S0 S3 T3 T0",
-            "B0 S1 T1 S2",
-            "C3 C1 T2 B3",
-            "B2 C0 G3 B1",
-            "C2 X3 G1 X1",
-            "G0 Y3 X0 G2",
-            "Y1 X2 H3 Y0",
-            "H1 Y2 H0 H2",
-            "E1 E0 N0 E3",
-            "E2 M1 M0 N1",
-            "M3 M2 N2 c1",
-            "N3 c0 A0 A1",
-            "c3 g1 x1 c2",
-            "g0 A2 x0 g3",
-            "y1 x3 g2 y0",
-            "x2 y3 h1 h0",
-            "y2 h3 h2 e0",
-            "O0 e1 O1 e3",
-            "A3 e2 O2 F1",
-            "F0 O3 F3 F2",
+            "S0 S1 T0 T1",
+            "B0 B1 S3 S2",
+            "C1 T3 T2 B2",
+            "C0 G1 C2 X1",
+            "C3 G0 B3 X0",
+            "Y1 G2 Y0 X2",
+            "H1 G3 X3 Y2",
+            "H0 E1 Y3 H2",
+            "N1 E0 H3 N0",
+            "M1 E2 M0 E3",
+            "c1 M2 c0 N2",
+            "M3 N3 g1 c2",
+            "A1 x1 g0 c3",
+            "x0 g2 y1 x2",
+            "g3 y0 x3 h1",
+            "y2 h0 y3 h2",
+            "A3 h3 A0 e0",
+            "e2 e1 e3 A2",
+            "O0 F0 O3 O1",
+            "F1 O2 F2 F3",
         ]
         return " ".join(order).split()
     return [f"{step}{j}" for step in "STBCGXYHENMAcgxyheOF" for j in range(chunks)]

time: 99 us -> 94.6 us (0.956)
  Pallas kernels: 93.8 us -> 90 us
    pallas_call x1, Pallas kernels: 93.8 us -> 90 us  [shards(): pl.pallas_call(functools.partial(kernel, ny, nx, nz, chunks), out_shape=(...]
where the time goes in v4:
time: 94.6 us; the launch traced here: 94.5 us
  Pallas kernels  90 us (95%)
  local copies, waits for them, and re-layouts  3.88 us (4%)
    pallas_call x1, Pallas kernels, shards(): pl.pallas_call(functools.partial(kernel, ny, nx, nz, chunks), out_shape=(...  90 us
    unnamed x4, local copies, waits for them, and re-layouts  3.88 us

profile of v4, /device:TPU:32, one launch (start us, length us, event | category | flops | bytes accessed | tf_op | source)
XLA Modules:
  0.0 94.5 jit_solution(16436737126920113205)
XLA Ops:
  0.6 90.0 %shard_map.84 = (bf16[128,4096]{1,0:T(8,128)(2,1)S(1)}, bf16[128,4096]{1,0:T(8,128)(2,1)S(1)}, bf16[128,4096]{1,0:T(8,128)(2,1)S(1)}, bf16[128,4096]{1,0:T(8,128)(2,1)S(1)}) custom-call(s32[8]{0:T(128)} %ids.1, bf16[128,4096]{1,0:T(8,128)(2,1)} %q_hbm.1, bf16[128,4096]{1,0:T(8,128)(2,1)} %k_hbm.1, bf16[128,4096]{1,0:T(8,128)(2,1)} %v_hbm.1, ...), custom_call_target="tpu_custom_call" | custom-call | tf_op jit(solution)/shard_map/pallas_call | solution.py:603
  90.6 1.0 %copy.13 = bf16[128,4096]{1,0:T(8,128)(2,1)} copy(bf16[128,4096]{1,0:T(8,128)(2,1)S(1)} %get-tuple-element.4) | data formatting | bytes 2097152
  91.6 1.0 %copy.14 = bf16[128,4096]{1,0:T(8,128)(2,1)} copy(bf16[128,4096]{1,0:T(8,128)(2,1)S(1)} %get-tuple-element.5) | data formatting | bytes 2097152
  92.5 1.0 %copy.15 = bf16[128,4096]{1,0:T(8,128)(2,1)} copy(bf16[128,4096]{1,0:T(8,128)(2,1)S(1)} %get-tuple-element.6) | data formatting | bytes 2097152
  93.5 1.0 %copy.16 = bf16[128,4096]{1,0:T(8,128)(2,1)} copy(bf16[128,4096]{1,0:T(8,128)(2,1)S(1)} %get-tuple-element.7) | data formatting | bytes 2097152
